TPU v7x, 128 devices: a whole 4x4x4 slice. The times are simulated.
128 devices in a mesh: pipe: 4 (over y), seq: 32 (over z, x, core).
Axes of the slice: x: 4, y: 4, z: 4, core: 2. Of those that a mesh axis runs over, the one named last changes fastest.
Arguments:
- hidden_in: bfloat16 [3072, 1536], P('seq'), may hold values from -6 to 6
- modulation: float32 [4, 3, 1536], P('pipe'), may hold values from -3 to 3
- w_qkv: bfloat16 [4, 1536, 4608], P('pipe'), may hold values from -0.15625 to 0.15625
- w_out: bfloat16 [4, 1536, 1536], P('pipe'), may hold values from -0.15625 to 0.15625
- qk_gain: float32 [4, 2, 128], P('pipe'), may hold values from 1.2 to 2.4
- stale_kv: bfloat16 [4, 3072, 2, 1536], P('pipe', 'seq'), may hold values from -6 to 6
- positions: int32 [3072, 3], P('seq'), may hold values from 0 to 63, as said below
- order: int32 [4], replicated, may hold values from 0 to 3, each once
Outputs:
- hidden_out: bfloat16 [4, 3072, 1536], P('pipe', 'seq')
- fresh_kv: bfloat16 [4, 3072, 2, 1536], P('pipe', 'seq')
Inputs may be any that keep to these rules, and one draw needn't show every extreme that they name: `positions`: distinct tokens have distinct (row, column); the text index is below 4, the row below 48 and the column below 64. `order`: each patch number once.
All inputs are finite; a program needn't handle non-finite values.
Results may differ from a plain program's by a relative error of at most 0.04.
Values may be sent and summed in bfloat16 or wider, within the bound.
No kernel may reach another device: no remote copies, remote signals or barrier semaphores. Data moves between devices by JAX's collectives and lax.ppermute only.
A program may use at most 64 MiB of HBM per device.

v0:
```python
import math

import jax
import jax.numpy as jnp
from jax import lax
from jax.sharding import PartitionSpec as P

HEAD_DIM = 128


def passed_along(value, axis, steps):
    count = lax.axis_size(axis)
    leading, last = (max(0, -steps), min(count, count - steps))
    return lax.ppermute(value, axis, [(source, source + steps) for source in range(leading, last)])


def rotary_tables(positions):
    pair_index = jnp.arange(64)
    axis_pick = jnp.where(pair_index < 8, 0, jnp.where(pair_index < 36, 1, 2))
    axis_start = jnp.where(pair_index < 8, 0, jnp.where(pair_index < 36, 8, 36))
    axis_width = jnp.where(pair_index < 8, 16.0, 56.0).astype(jnp.float32)
    inner_index = (pair_index - axis_start).astype(jnp.float32)
    frequency = jnp.power(jnp.float32(10000.0), -2.0 * inner_index / axis_width)
    one_hot = (jnp.arange(3)[:, None] == axis_pick[None, :]).astype(jnp.float32)
    coords = positions.astype(jnp.float32)
    picked = jnp.sum(coords[:, :, None] * one_hot[None, :, :], axis=1)
    angles = picked * frequency[None, :]
    return (jnp.cos(angles), jnp.sin(angles))


def rotate(heads_in, cosine, sine_part):
    shaped = heads_in.reshape(heads_in.shape[0], heads_in.shape[1], 64, 2)
    even_part = shaped[..., 0]
    odd_part = shaped[..., 1]
    cos_rows = cosine[:, None, :]
    sin_rows = sine_part[:, None, :]
    turned = jnp.stack(
        [cos_rows * even_part - sin_rows * odd_part, sin_rows * even_part + cos_rows * odd_part],
        axis=-1,
    )
    return turned.reshape(heads_in.shape)


def head_norm(heads_in, gain_row):
    return (
        heads_in
        * (1.0 / jnp.sqrt(jnp.mean(heads_in * heads_in, axis=-1, keepdims=True) + 1e-06))
        * gain_row
    )


def modulate(hidden, shift_row, scale_row):
    values = hidden.astype(jnp.float32)
    centred = values - jnp.mean(values, axis=-1, keepdims=True)
    spread = jnp.mean(centred * centred, axis=-1, keepdims=True)
    return (centred / jnp.sqrt(spread + 1e-06) * (1.0 + scale_row) + shift_row).astype(jnp.bfloat16)


def on_device(hidden_in, modulation, w_qkv, w_out, qk_gain, stale_kv, positions, order):
    sections = lax.axis_size("pipe")
    section_index = lax.axis_index("pipe")
    seq_index = lax.axis_index("seq")
    tok_dev = hidden_in.shape[0]
    feature_count = hidden_in.shape[1]
    patches = order.shape[0]
    patch_dev = tok_dev // patches
    width_heads = w_out.shape[1]
    head_count = width_heads // HEAD_DIM
    scale_factor = 1.0 / math.sqrt(HEAD_DIM)
    shift_row = modulation[0, 0]
    scale_row = modulation[0, 1]
    gate_row = modulation[0, 2]
    weight_in = w_qkv[0]
    weight_out = w_out[0]
    query_gain = qk_gain[0, 0]
    key_gain = qk_gain[0, 1]
    cos_all, sin_all = rotary_tables(positions)

    def key_hats(raw_rows, cos_rows, sin_rows):
        shaped = raw_rows[:, 0].astype(jnp.float32).reshape(raw_rows.shape[0], head_count, HEAD_DIM)
        return rotate(head_norm(shaped, key_gain), cos_rows, sin_rows).astype(jnp.bfloat16)

    raw_start = stale_kv[0]
    hats_start = jnp.zeros((1, head_count, HEAD_DIM), jnp.bfloat16)

    def advance(turn_index, state_in):
        received, raw_buf, hats_buf, out_buf = state_in
        rank_index = turn_index - section_index
        is_active = jnp.logical_and(rank_index >= 0, rank_index < patches)
        patch_id = order[jnp.clip(rank_index, 0, patches - 1)]
        row_start = patch_id * patch_dev
        own_rows = lax.dynamic_slice_in_dim(hidden_in, row_start, patch_dev, 0)
        rows_in = jnp.where(section_index == 0, own_rows, received)
        modulated = modulate(rows_in, shift_row, scale_row)
        projected = jnp.dot(modulated, weight_in, preferred_element_type=jnp.float32)
        cos_rows = lax.dynamic_slice_in_dim(cos_all, row_start, patch_dev, 0)
        sin_rows = lax.dynamic_slice_in_dim(sin_all, row_start, patch_dev, 0)
        query_raw = projected[:, :width_heads].reshape(patch_dev, head_count, HEAD_DIM)
        query_hat = rotate(head_norm(query_raw, query_gain), cos_rows, sin_rows).astype(
            jnp.bfloat16
        )
        query_hat = query_hat.reshape(patch_dev, width_heads)
        fresh_pair = jnp.stack(
            [projected[:, width_heads : 2 * width_heads], projected[:, 2 * width_heads :]], axis=1
        ).astype(jnp.bfloat16)
        old_raw = lax.dynamic_slice_in_dim(raw_buf, row_start, patch_dev, 0)
        raw_buf = lax.dynamic_update_slice_in_dim(
            raw_buf, jnp.where(is_active, fresh_pair, old_raw), row_start, 0
        )
        key_all = key_hats(raw_buf, cos_all, sin_all)
        gathered = lax.all_gather(query_hat, "seq", axis=0, tiled=True)
        patch_tokens = gathered.shape[0]
        scores = (
            jnp.einsum(
                "qhd,khd->hqk",
                gathered.reshape(patch_tokens, head_count, HEAD_DIM),
                key_all,
                preferred_element_type=jnp.float32,
            )
            * scale_factor
        )
        weights = jnp.exp(scores)
        partial_den = jnp.transpose(jnp.sum(weights, axis=2))
        value_rows = raw_buf[:, 1].reshape(tok_dev, head_count, HEAD_DIM)
        partial_num = jnp.einsum(
            "hqk,khd->qhd",
            weights.astype(jnp.bfloat16),
            value_rows,
            preferred_element_type=jnp.float32,
        )
        partial_num = partial_num.reshape(patch_tokens, width_heads)
        numerator = lax.psum_scatter(
            partial_num.astype(jnp.bfloat16), "seq", scatter_dimension=0, tiled=True
        ).astype(jnp.float32)
        summed = lax.psum(partial_den.astype(jnp.bfloat16), "seq").astype(jnp.float32)
        denominator = lax.dynamic_slice_in_dim(summed, seq_index * patch_dev, patch_dev, 0)
        attended = (
            numerator.reshape(patch_dev, head_count, HEAD_DIM) / denominator[:, :, None]
        ).astype(jnp.bfloat16)
        branch_out = jnp.dot(
            attended.reshape(patch_dev, width_heads), weight_out, preferred_element_type=jnp.float32
        )
        new_rows = (rows_in.astype(jnp.float32) + gate_row * branch_out).astype(jnp.bfloat16)
        old_out = lax.dynamic_slice_in_dim(out_buf, row_start, patch_dev, 0)
        out_buf = lax.dynamic_update_slice_in_dim(
            out_buf, jnp.where(is_active, new_rows, old_out), row_start, 0
        )
        passed = passed_along(new_rows, "pipe", 1)
        return (passed, raw_buf, hats_buf, out_buf)

    start_state = (
        jnp.zeros((patch_dev, feature_count), jnp.bfloat16),
        raw_start,
        hats_start,
        jnp.zeros((tok_dev, feature_count), jnp.bfloat16),
    )
    final_state = lax.fori_loop(0, patches + sections - 1, advance, start_state)
    return (final_state[3][None], final_state[1][None])


def solution(mesh):
    in_specs = (
        P("seq", None),
        P("pipe", None, None),
        P("pipe", None, None),
        P("pipe", None, None),
        P("pipe", None, None),
        P("pipe", "seq", None, None),
        P("seq", None),
        P(),
    )
    out_specs = (P("pipe", "seq", None), P("pipe", "seq", None, None))
    return jax.shard_map(
        on_device, mesh=mesh, in_specs=in_specs, out_specs=out_specs, check_vma=False
    )
```

profile of v0, /device:TPU:24, one launch (start us, length us, event | category | flops | bytes accessed | tf_op | source)
XLA Modules:
  0.0 1437.8 jit_solution(3507462731914099478)
XLA Ops:
  12.1 1417.7 %while.19 = (s32[]{:T(128)}, bf16[24,1536]{1,0:T(8,128)(2,1)S(1)}, bf16[96,2,1536]{2,0,1:T(8,128)(2,1)S(1)}, bf16[96,1536]{1,0:T(8,128)(2,1)}, pred[]{:T(512)}, ...) while((s32[]{:T(128)}, bf16[24,1536]{1,0:T(8,128)(2,1)S(1)}, ...), condition=%wide.region_9.10_spmd, body=%wide.region_1.9_spmd.sunk | while | flops 914451712 | bytes 71067952 | solution.py:157
  16.6 7.0 fusion.58
  29.3 5.6 dynamic_update_slice.22
  38.3 35.9 %all-gather.2.cloned.1.call-done = bf16[768,1536]{1,0:T(8,128)(2,1)} async-done(((bf16[24,1536]{1,0:T(8,128)(2,1)}), bf16[768,1536]{1,0:T(8,128)(2,1)}) %all-gather.2.cloned.1.call-update) | async-done | bytes 2359312 | tf_op jit(solution)/shard_map/while/body/eval_jaxpr/all_gather | solution.py:111
  82.0 126.3 %psum.14 = bf16[768,12]{0,1:T(8,128)(2,1)S(1)} all-reduce(bf16[768,12]{0,1:T(8,128)(2,1)S(1)} %bitcast.89), channel_id=1, replica_groups=mesh['pipe'=4,'seq'=32] {'seq'}, use_global_device_ids=true, to_apply=%region_8.8 | all-reduce | flops 9216 | bytes 36864 | tf_op jit(solution)/shard_map/while/body/eval_jaxpr/psum | solution.py:135
  224.2 7.0 fusion.58
  236.8 5.6 dynamic_update_slice.22
  245.8 30.1 %all-gather.2.cloned.1.call-done = bf16[768,1536]{1,0:T(8,128)(2,1)} async-done(((bf16[24,1536]{1,0:T(8,128)(2,1)}), bf16[768,1536]{1,0:T(8,128)(2,1)}) %all-gather.2.cloned.1.call-update) | async-done | bytes 2359312 | tf_op jit(solution)/shard_map/while/body/eval_jaxpr/all_gather | solution.py:111
  283.7 126.5 %psum.14 = bf16[768,12]{0,1:T(8,128)(2,1)S(1)} all-reduce(bf16[768,12]{0,1:T(8,128)(2,1)S(1)} %bitcast.89), channel_id=1, replica_groups=mesh['pipe'=4,'seq'=32] {'seq'}, use_global_device_ids=true, to_apply=%region_8.8 | all-reduce | flops 9216 | bytes 36864 | tf_op jit(solution)/shard_map/while/body/eval_jaxpr/psum | solution.py:135
  426.1 7.0 fusion.58
  447.7 29.9 %all-gather.2.cloned.1.call-done = bf16[768,1536]{1,0:T(8,128)(2,1)} async-done(((bf16[24,1536]{1,0:T(8,128)(2,1)}), bf16[768,1536]{1,0:T(8,128)(2,1)}) %all-gather.2.cloned.1.call-update) | async-done | bytes 2359312 | tf_op jit(solution)/shard_map/while/body/eval_jaxpr/all_gather | solution.py:111
  485.3 126.3 %psum.14 = bf16[768,12]{0,1:T(8,128)(2,1)S(1)} all-reduce(bf16[768,12]{0,1:T(8,128)(2,1)S(1)} %bitcast.89), channel_id=1, replica_groups=mesh['pipe'=4,'seq'=32] {'seq'}, use_global_device_ids=true, to_apply=%region_8.8 | all-reduce | flops 9216 | bytes 36864 | tf_op jit(solution)/shard_map/while/body/eval_jaxpr/psum | solution.py:135
  627.6 7.0 fusion.58
  649.2 30.1 %all-gather.2.cloned.1.call-done = bf16[768,1536]{1,0:T(8,128)(2,1)} async-done(((bf16[24,1536]{1,0:T(8,128)(2,1)}), bf16[768,1536]{1,0:T(8,128)(2,1)}) %all-gather.2.cloned.1.call-update) | async-done | bytes 2359312 | tf_op jit(solution)/shard_map/while/body/eval_jaxpr/all_gather | solution.py:111
  687.0 126.3 %psum.14 = bf16[768,12]{0,1:T(8,128)(2,1)S(1)} all-reduce(bf16[768,12]{0,1:T(8,128)(2,1)S(1)} %bitcast.89), channel_id=1, replica_groups=mesh['pipe'=4,'seq'=32] {'seq'}, use_global_device_ids=true, to_apply=%region_8.8 | all-reduce | flops 9216 | bytes 36864 | tf_op jit(solution)/shard_map/while/body/eval_jaxpr/psum | solution.py:135
  829.3 7.0 fusion.58
  850.9 30.1 %all-gather.2.cloned.1.call-done = bf16[768,1536]{1,0:T(8,128)(2,1)} async-done(((bf16[24,1536]{1,0:T(8,128)(2,1)}), bf16[768,1536]{1,0:T(8,128)(2,1)}) %all-gather.2.cloned.1.call-update) | async-done | bytes 2359312 | tf_op jit(solution)/shard_map/while/body/eval_jaxpr/all_gather | solution.py:111
  888.7 126.3 %psum.14 = bf16[768,12]{0,1:T(8,128)(2,1)S(1)} all-reduce(bf16[768,12]{0,1:T(8,128)(2,1)S(1)} %bitcast.89), channel_id=1, replica_groups=mesh['pipe'=4,'seq'=32] {'seq'}, use_global_device_ids=true, to_apply=%region_8.8 | all-reduce | flops 9216 | bytes 36864 | tf_op jit(solution)/shard_map/while/body/eval_jaxpr/psum | solution.py:135
  1031.0 7.0 fusion.58
  1050.1 32.6 %all-gather.2.cloned.1.call-done = bf16[768,1536]{1,0:T(8,128)(2,1)} async-done(((bf16[24,1536]{1,0:T(8,128)(2,1)}), bf16[768,1536]{1,0:T(8,128)(2,1)}) %all-gather.2.cloned.1.call-update) | async-done | bytes 2359312 | tf_op jit(solution)/shard_map/while/body/eval_jaxpr/all_gather | solution.py:111
  1090.4 126.5 %psum.14 = bf16[768,12]{0,1:T(8,128)(2,1)S(1)} all-reduce(bf16[768,12]{0,1:T(8,128)(2,1)S(1)} %bitcast.89), channel_id=1, replica_groups=mesh['pipe'=4,'seq'=32] {'seq'}, use_global_device_ids=true, to_apply=%region_8.8 | all-reduce | flops 9216 | bytes 36864 | tf_op jit(solution)/shard_map/while/body/eval_jaxpr/psum | solution.py:135
  1232.9 7.0 fusion.58
  1254.5 29.9 %all-gather.2.cloned.1.call-done = bf16[768,1536]{1,0:T(8,128)(2,1)} async-done(((bf16[24,1536]{1,0:T(8,128)(2,1)}), bf16[768,1536]{1,0:T(8,128)(2,1)}) %all-gather.2.cloned.1.call-update) | async-done | bytes 2359312 | tf_op jit(solution)/shard_map/while/body/eval_jaxpr/all_gather | solution.py:111
  1292.1 126.3 %psum.14 = bf16[768,12]{0,1:T(8,128)(2,1)S(1)} all-reduce(bf16[768,12]{0,1:T(8,128)(2,1)S(1)} %bitcast.89), channel_id=1, replica_groups=mesh['pipe'=4,'seq'=32] {'seq'}, use_global_device_ids=true, to_apply=%region_8.8 | all-reduce | flops 9216 | bytes 36864 | tf_op jit(solution)/shard_map/while/body/eval_jaxpr/psum | solution.py:135
  (556 shorter events, 252.6 us)
Async XLA Ops:
  12.2 62.1 %all-gather.2.cloned.1.call-start = ((), (), s32[]{:S(2)}) async-start(), calls=%async_computation.1 | async-start | bytes 2433024 | tf_op jit(solution)/shard_map/while/body/eval_jaxpr/all_gather | solution.py:111
  27.6 180.7 %reduce-scatter.6.cloned.1.call-start = ((), (), s32[]{:S(2)}) async-start(), calls=%async_computation.2 | async-start | bytes 2433024 | tf_op jit(solution)/shard_map/while
  213.4 6.2 collective-permute-start
  219.7 56.2 %all-gather.2.cloned.1.call-start = ((), (), s32[]{:S(2)}) async-start(), calls=%async_computation.1 | async-start | bytes 2433024 | tf_op jit(solution)/shard_map/while/body/eval_jaxpr/all_gather | solution.py:111
  235.2 175.1 %reduce-scatter.6.cloned.1.call-start = ((), (), s32[]{:S(2)}) async-start(), calls=%async_computation.2 | async-start | bytes 2433024 | tf_op jit(solution)/shard_map/while
  281.1 130.4 %copy-start.2 = (bf16[24,1536]{1,0:T(8,128)(2,1)S(1)}, bf16[24,1536]{1,0:T(8,128)(2,1)}, u32[]{:S(2)}) copy-start(bf16[24,1536]{1,0:T(8,128)(2,1)} %copy-done.1) | copy-start | bytes 221188 | tf_op jit(solution)/shard_map/while
  415.3 6.2 collective-permute-start
  421.6 56.0 %all-gather.2.cloned.1.call-start = ((), (), s32[]{:S(2)}) async-start(), calls=%async_computation.1 | async-start | bytes 2433024 | tf_op jit(solution)/shard_map/while/body/eval_jaxpr/all_gather | solution.py:111
  437.1 174.7 %reduce-scatter.6.cloned.1.call-start = ((), (), s32[]{:S(2)}) async-start(), calls=%async_computation.2 | async-start | bytes 2433024 | tf_op jit(solution)/shard_map/while
  616.8 6.2 collective-permute-start
  623.1 56.2 %all-gather.2.cloned.1.call-start = ((), (), s32[]{:S(2)}) async-start(), calls=%async_computation.1 | async-start | bytes 2433024 | tf_op jit(solution)/shard_map/while/body/eval_jaxpr/all_gather | solution.py:111
  638.6 174.9 %reduce-scatter.6.cloned.1.call-start = ((), (), s32[]{:S(2)}) async-start(), calls=%async_computation.2 | async-start | bytes 2433024 | tf_op jit(solution)/shard_map/while
  684.5 130.2 %copy-start.2 = (bf16[24,1536]{1,0:T(8,128)(2,1)S(1)}, bf16[24,1536]{1,0:T(8,128)(2,1)}, u32[]{:S(2)}) copy-start(bf16[24,1536]{1,0:T(8,128)(2,1)} %copy-done.1) | copy-start | bytes 221188 | tf_op jit(solution)/shard_map/while
  818.5 6.2 collective-permute-start
  824.8 56.2 %all-gather.2.cloned.1.call-start = ((), (), s32[]{:S(2)}) async-start(), calls=%async_computation.1 | async-start | bytes 2433024 | tf_op jit(solution)/shard_map/while/body/eval_jaxpr/all_gather | solution.py:111
  840.3 174.9 %reduce-scatter.6.cloned.1.call-start = ((), (), s32[]{:S(2)}) async-start(), calls=%async_computation.2 | async-start | bytes 2433024 | tf_op jit(solution)/shard_map/while
  1020.2 6.2 collective-permute-start
  1026.5 56.2 %all-gather.2.cloned.1.call-start = ((), (), s32[]{:S(2)}) async-start(), calls=%async_computation.1 | async-start | bytes 2433024 | tf_op jit(solution)/shard_map/while/body/eval_jaxpr/all_gather | solution.py:111
  1042.0 175.1 %reduce-scatter.6.cloned.1.call-start = ((), (), s32[]{:S(2)}) async-start(), calls=%async_computation.2 | async-start | bytes 2433024 | tf_op jit(solution)/shard_map/while
  1087.9 130.4 %copy-start.2 = (bf16[24,1536]{1,0:T(8,128)(2,1)S(1)}, bf16[24,1536]{1,0:T(8,128)(2,1)}, u32[]{:S(2)}) copy-start(bf16[24,1536]{1,0:T(8,128)(2,1)} %copy-done.1) | copy-start | bytes 221188 | tf_op jit(solution)/shard_map/while
  1222.1 6.2 collective-permute-start
  1228.4 56.0 %all-gather.2.cloned.1.call-start = ((), (), s32[]{:S(2)}) async-start(), calls=%async_computation.1 | async-start | bytes 2433024 | tf_op jit(solution)/shard_map/while/body/eval_jaxpr/all_gather | solution.py:111
  1243.8 174.7 %reduce-scatter.6.cloned.1.call-start = ((), (), s32[]{:S(2)}) async-start(), calls=%async_computation.2 | async-start | bytes 2433024 | tf_op jit(solution)/shard_map/while
  1423.5 6.2 collective-permute-start
  (88 other events, 1362.7 us)
Sparse Core Ops, SparseCore 0:
  27.8 46.4 all-gather.1
  82.0 78.5 reduce-scatter.5
  235.3 40.5 all-gather.1
  283.7 78.6 reduce-scatter.5
  437.2 40.3 all-gather.1
  485.4 78.5 reduce-scatter.5
  638.7 40.5 all-gather.1
  687.1 78.5 reduce-scatter.5
  840.4 40.5 all-gather.1
  888.8 78.5 reduce-scatter.5
  1042.1 40.5 all-gather.1
  1090.5 78.6 reduce-scatter.5
  1244.0 40.3 all-gather.1
  1292.2 78.5 reduce-scatter.5
where the time goes:
time: 1440 us
  blocking collectives  885 us (61%)
  waiting for transfers between devices  251 us (17%)
  local copies, waits for them, and re-layouts  117 us (8%)
  matrix products  91.8 us (6%)
  other arithmetic  61.9 us (4%)
    psum x7, blocking collectives, advance(): lax.psum(partial_den.astype(jnp.bfloat16), 'seq').astype(jnp.float32)  885 us
    all_gather x7, waiting for transfers between devices, advance(): gathered = lax.all_gather(query_hat, 'seq', axis=0, tiled=True)  218 us
    dot_general x7, matrix products, advance(): jnp.dot(modulated, weight_in, preferred_element_type=jnp.float32)  49.2 us
    dynamic_update_slice x7, local copies, waits for them, and re-layouts, advance(): lax.dynamic_update_slice_in_dim(raw_buf, jnp.where(is_active, fresh_pair,...  36.4 us
    ppermute x7, waiting for transfers between devices, passed_along(): lax.ppermute(value, axis, [(source, source + steps) for source in range(l...  32.7 us
  transfers between devices with their start and end apart: 21, of which 14 were waited for; matrix products, arithmetic and copies ran while one was open for 5% of the time, Pallas kernels for 0%

commit v1 on v0

v1 whole, which is shorter than its diff:
```python
import functools
import math

import jax
import jax.numpy as jnp
import numpy as np
from jax import lax
from jax.experimental import pallas as pl
from jax.experimental.pallas import tpu as pltpu
from jax.sharding import Mesh
from jax.sharding import PartitionSpec as P

GROUPS = 2
PATCHES = 4
HEAD = 128
HEADS = 12
CHIPS = 16
PD = 24
D = 1536
LAYERS = 4
PER = PATCHES // GROUPS
N = PER * PD
KEYS = 2 * CHIPS * PD
F32 = jnp.float32
BF16 = jnp.bfloat16


def rotary_tables(positions):
    lane = np.arange(HEAD)
    pair = lane // 2
    axis = np.where(pair < 8, 0, np.where(pair < 36, 1, 2))
    start = np.where(pair < 8, 0, np.where(pair < 36, 8, 36))
    width = np.where(pair < 8, 16.0, 56.0)
    freq = jnp.asarray(np.power(10000.0, -2.0 * (pair - start) / width).astype(np.float32))[None]
    c = positions.astype(F32)
    picked = jnp.where(axis[None] == 0, c[:, 0:1], jnp.where(axis[None] == 1, c[:, 1:2], c[:, 2:3]))
    angle = picked * freq
    cos, sin = jnp.cos(angle), jnp.sin(angle)
    even = (lane % 2 == 0)[None]
    down = jnp.where(even, -sin, 0.0)
    up = jnp.where(even, 0.0, sin)
    return jnp.concatenate([cos, down, up], axis=1).reshape(PATCHES, PD, 3 * HEAD)


def hats(x, gain, tab):
    inv = lax.rsqrt(jnp.mean(x * x, axis=-1, keepdims=True) + 1e-6)
    x = x * inv * gain
    return (
        x * tab[:, :HEAD]
        + pltpu.roll(x, HEAD - 1, 1) * tab[:, HEAD : 2 * HEAD]
        + pltpu.roll(x, 1, 1) * tab[:, 2 * HEAD :]
    )


def stage(info_ref, turn):
    section = info_ref[0]
    g = jnp.clip(turn - section, 0, GROUPS - 1)
    ids = [info_ref[1 + g * PER + j] for j in range(PER)]
    return section, g, ids


def rows_of(info_ref, turn, x_ref, recv_ref):
    section, _, ids = stage(info_ref, turn)
    own = jnp.concatenate([x_ref[p].astype(F32) for p in ids], axis=0)
    if recv_ref is None:
        return own
    return jnp.where(section == 0, own, recv_ref[...].astype(F32))


def project_kernel(turn, *refs):
    first = turn == 0
    refs = list(refs)
    info_ref, x_ref = refs[:2]
    refs = refs[2:]
    recv_ref = None if first else refs.pop(0)
    mod_ref, w_ref, gain_ref, tab_ref = refs[:4]
    refs = refs[4:]
    stale_ref = refs.pop(0) if first else None
    chunk_ref, fresh_ref = refs
    _, _, ids = stage(info_ref, turn)
    rows = rows_of(info_ref, turn, x_ref, recv_ref)
    centred = rows - jnp.mean(rows, axis=-1, keepdims=True)
    spread = jnp.mean(centred * centred, axis=-1, keepdims=True)
    modulated = (
        centred * lax.rsqrt(spread + 1e-6) * (1.0 + mod_ref[0, 1:2, :]) + mod_ref[0, 0:1, :]
    ).astype(BF16)
    q_gain = gain_ref[0, 0:1, :] * (math.log2(math.e) / math.sqrt(HEAD))
    k_gain = gain_ref[0, 1:2, :]
    tab = jnp.concatenate([tab_ref[p] for p in ids], axis=0)
    wide = 4 * HEAD
    for block in range(D // wide):
        q, k, v = (
            jnp.dot(
                modulated,
                w_ref[0, :, part * D + block * wide : part * D + (block + 1) * wide],
                preferred_element_type=F32,
            )
            for part in range(3)
        )
        k16, v16 = k.astype(BF16), v.astype(BF16)
        fresh_ref[:, block * wide : (block + 1) * wide] = k16
        fresh_ref[:, D + block * wide : D + (block + 1) * wide] = v16
        k, v = k16.astype(F32), v16.astype(F32)
        for i in range(wide // HEAD):
            h = block * (wide // HEAD) + i
            lanes = slice(i * HEAD, (i + 1) * HEAD)
            qh = hats(q[:, lanes], q_gain, tab)
            kh = hats(k[:, lanes], k_gain, tab)
            vh = v[:, lanes]
            parts = []
            for j in range(PER):
                here = slice(PD * j, PD * (j + 1))
                parts += [qh[here], kh[here], vh[here]]
            if first:
                for r in range(1, PATCHES):
                    p = info_ref[1 + r]
                    ks = stale_ref[p, :, h * HEAD : (h + 1) * HEAD].astype(F32)
                    vs = stale_ref[p, :, D + h * HEAD : D + (h + 1) * HEAD].astype(F32)
                    parts += [hats(ks, k_gain, tab_ref[p]), vs]
            chunk_ref[h] = jnp.concatenate(parts, axis=0).astype(BF16)
    for c in range(HEADS, CHIPS):
        chunk_ref[c] = jnp.zeros(chunk_ref.shape[1:], BF16)


def attend_kernel(turn, last, *refs):
    first = turn == 0
    refs = list(refs)
    info_ref, own_ref, oth_ref = refs[:3]
    refs = refs[3:]
    kin_ref, vin_ref = (None, None) if first else (refs.pop(0), refs.pop(0))
    out_ref = refs.pop(0)
    kout_ref, vout_ref = (None, None) if last else (refs.pop(0), refs.pop(0))
    kown_ref, vown_ref = refs
    section, g, _ = stage(info_ref, turn)
    own = own_ref[...].astype(F32)
    oth = oth_ref[...].astype(F32)

    def pick(x, start):
        return x[:, start : start + PD, :].reshape(CHIPS * PD, HEAD)

    def both(start):
        return jnp.concatenate([pick(own, start), pick(oth, start)], axis=0).astype(BF16)

    if first:
        kin_ref, vin_ref = kout_ref, vout_ref
        for r in range(1, PATCHES):
            start = PER * 3 * PD + (r - 1) * 2 * PD
            kin_ref[r] = both(start)
            vin_ref[r] = both(start + PD)
        base = 0
    else:
        base = g * PER
    ones = jnp.ones((KEYS, HEAD), BF16)
    outs = []
    for j in range(PER):
        kown_ref[j] = both(3 * PD * j + PD)
        vown_ref[j] = both(3 * PD * j + 2 * PD)
        q = pick(own, 3 * PD * j).astype(BF16)
        total = jnp.zeros((CHIPS * PD, 2 * HEAD), F32)
        for i in range(PATCHES):
            if i <= j:
                k, v = kown_ref[i], vown_ref[i]
            else:
                n = i - j - 1
                slot = n + j + 1 if first else jnp.where(n < base, n, n + j + 1)
                k, v = kin_ref[slot], vin_ref[slot]
            s = lax.dot_general(q, k, (((1,), (1,)), ((), ())), preferred_element_type=F32)
            w = jnp.exp2(s).astype(BF16)
            total = total + jnp.dot(
                w, jnp.concatenate([v, ones], axis=1), preferred_element_type=F32
            )
        att = total[:, :HEAD] / total[:, HEAD:]
        outs.append(att.reshape(CHIPS, PD, HEAD))
    out_ref[...] = jnp.concatenate(outs, axis=1).astype(BF16)
    if last:
        return
    begun = turn >= section
    if not first:
        for n in range(PATCHES - PER):
            slot = jnp.where(n < base, n, n + PER)
            kout_ref[slot] = kin_ref[slot]
            vout_ref[slot] = vin_ref[slot]
    elif PER < PATCHES:
        kin_ref[0] = kown_ref[0]
        vin_ref[0] = vown_ref[0]
    for j in range(PER):
        kout_ref[base + j] = jnp.where(begun, kown_ref[j], kin_ref[base + j])
        vout_ref[base + j] = jnp.where(begun, vown_ref[j], vin_ref[base + j])


def output_kernel(turn, last, *refs):
    first = turn == 0
    refs = list(refs)
    info_ref, att_ref, w_ref, x_ref = refs[:4]
    refs = refs[4:]
    recv_ref = None if first else refs.pop(0)
    mod_ref = refs.pop(0)
    att = jnp.concatenate([att_ref[h] for h in range(HEADS)], axis=1)
    rows = rows_of(info_ref, turn, x_ref, recv_ref)
    branch = jnp.dot(att, w_ref[0], preferred_element_type=F32)
    new = rows + mod_ref[0, 2:3, :] * branch
    if not last:
        refs[0][...] = new.astype(BF16)
        return
    *olds, out_ref = refs
    for section in range(LAYERS):

        @pl.when(info_ref[0] == section)
        def _():
            for g in range(GROUPS):
                rows = new if section + g == turn else olds[section + g][...].astype(F32)
                for j in range(PER):
                    p = info_ref[1 + g * PER + j]
                    out_ref[p] = rows[PD * j : PD * (j + 1)].astype(BF16)


def collect_kernel(info_ref, *refs):
    *olds, out_ref = refs
    for section in range(LAYERS):

        @pl.when(info_ref[0] == section)
        def _():
            for g in range(GROUPS):
                rows = olds[section + g][...].astype(F32)
                for j in range(PER):
                    p = info_ref[1 + g * PER + j]
                    out_ref[p] = rows[PD * j : PD * (j + 1)].astype(BF16)


SMEM = pl.BlockSpec(memory_space=pltpu.SMEM)
VMEM = pl.BlockSpec(memory_space=pltpu.VMEM)


def shape(*dims, dtype=BF16):
    return jax.ShapeDtypeStruct(dims, dtype)


def call(kernel, name, out_shape, args, limit, scratch=()):
    return pl.pallas_call(
        kernel,
        out_shape=out_shape,
        in_specs=[SMEM] + [VMEM] * (len(args) - 1),
        out_specs=[VMEM] * len(out_shape),
        scratch_shapes=list(scratch),
        compiler_params=pltpu.CompilerParams(vmem_limit_bytes=limit * 2**20),
        name=name,
    )(*args)


def on_device(hidden_in, modulation, w_qkv, w_out, qk_gain, stale_kv, positions, order):
    section = lax.axis_index("pipe")
    info = jnp.concatenate([jnp.stack([section]).astype(jnp.int32), order])
    x = hidden_in.reshape(PATCHES, PD, D)
    stale = stale_kv[0].reshape(PATCHES, PD, 2 * D)
    tab = rotary_tables(positions)
    turns = GROUPS + LAYERS - 1
    recv = kbuf = vbuf = None
    fresh, hidden = [], []
    for turn in range(turns):
        first, last = turn == 0, turn == turns - 1
        rows = PER * 3 * PD + (3 * 2 * PD if first else 0)
        args = [info, x] + ([] if first else [recv]) + [modulation, w_qkv, qk_gain, tab]
        args += [stale] if first else []
        chunk, raw = call(
            functools.partial(project_kernel, turn),
            f"project{turn}",
            [shape(CHIPS, rows, HEAD), shape(N, 2 * D)],
            args,
            20,
        )
        fresh.append(raw)
        own = lax.all_to_all(chunk, ("z", "x"), 0, 0, tiled=True)
        oth = lax.ppermute(own, "core", [(0, 1), (1, 0)])
        buf = shape(PATCHES, KEYS, HEAD)
        att, *bufs = call(
            functools.partial(attend_kernel, turn, last),
            f"attend{turn}",
            [shape(CHIPS, N, HEAD)] + ([] if last else [buf, buf]),
            [info, own, oth] + ([] if first else [kbuf, vbuf]),
            20,
            [pltpu.VMEM((PER, KEYS, HEAD), BF16)] * 2,
        )
        back = lax.all_to_all(att, ("z", "x"), 0, 0, tiled=True)
        args = [info, back, w_out, x] + ([] if first else [recv]) + [modulation]
        (new,) = call(
            functools.partial(output_kernel, turn, last),
            f"output{turn}",
            [shape(PATCHES, PD, D) if last else shape(N, D)],
            args + (hidden if last else []),
            20,
        )
        hidden.append(new)
        if not last:
            kbuf, vbuf = bufs
            recv = lax.ppermute(new, "pipe", [(i, i + 1) for i in range(LAYERS - 1)])
    (kept,) = call(collect_kernel, "collect", [shape(PATCHES, PD, 2 * D)], [info] + fresh, 20)
    return (hidden[-1].reshape(1, PATCHES * PD, D), kept.reshape(1, PATCHES * PD, 2, D))


def solution(mesh):
    fine = Mesh(mesh.devices.reshape(4, 4, 4, 2), ("pipe", "z", "x", "core"))
    seq = ("z", "x", "core")
    in_specs = (
        P(seq, None),
        P("pipe", None, None),
        P("pipe", None, None),
        P("pipe", None, None),
        P("pipe", None, None),
        P("pipe", seq, None, None),
        P(seq, None),
        P(),
    )
    out_specs = (P("pipe", seq, None), P("pipe", seq, None, None))
    return jax.shard_map(
        on_device, mesh=fine, in_specs=in_specs, out_specs=out_specs, check_vma=False
    )
```

time: 1440 us -> 238 us (0.17)
  blocking collectives: 885 us -> 126 us
  waiting for transfers between devices: 251 us -> 40.5 us
  local copies, waits for them, and re-layouts: 117 us -> 11.9 us
  matrix products: 91.8 us -> 0 us
  other arithmetic: 61.9 us -> 1.11 us
  Pallas kernels: 0 us -> 47.7 us
    psum x7 -> x0, blocking collectives: 885 us -> none  [advance(): lax.psum(partial_den.astype(jnp.bfloat16), 'seq').astype(jnp.float32)]
    all_gather x7 -> x0, waiting for transfers between devices: 218 us -> none  [advance(): gathered = lax.all_gather(query_hat, 'seq', axis=0, tiled=True)]
    all_to_all x0 -> x9, blocking collectives: none -> 126 us  [the longest x5 80.1 us: on_device(): own = lax.all_to_all(chunk, ('z', 'x'), 0, 0, tiled=True)]
    dot_general x28 -> x0, matrix products: 91.8 us -> none  [the longest x7 49.2 us: advance(): jnp.dot(modulated, weight_in, preferred_element_type=jnp.float32)]
    pallas_call x0 -> x16, Pallas kernels: none -> 47.7 us  [call(): pl.pallas_call(kernel, out_shape=out_shape, in_specs=[SMEM] + [VMEM] * (l...]
    another operation x56 -> x0, other arithmetic: 37.3 us -> none
    dynamic_update_slice x7 -> x0, local copies, waits for them, and re-layouts: 36.4 us -> none  [advance(): lax.dynamic_update_slice_in_dim(raw_buf, jnp.where(is_active, fresh_pair,...]
    while x197 -> x0, local copies, waits for them, and re-layouts: 26.7 us -> none
  transfers between devices with their start and end apart: 21 -> 10, of which waited for: 14 -> 10; matrix products, arithmetic and copies ran while one was open for 5% -> 1% of each run, Pallas kernels for 0% -> 0%
where the time goes in v1:
time: 238 us; the launch traced here: 237 us
  blocking collectives  126 us (53%)
  Pallas kernels  47.7 us (20%)
  waiting for transfers between devices  40.5 us (17%)
  local copies, waits for them, and re-layouts  11.9 us (5%)
  starting transfers between devices  8.7 us (4%)
    all_to_all x5, blocking collectives, on_device(): own = lax.all_to_all(chunk, ('z', 'x'), 0, 0, tiled=True)  80.1 us
    pallas_call x16, Pallas kernels, call(): pl.pallas_call(kernel, out_shape=out_shape, in_specs=[SMEM] + [VMEM] * (l...  47.7 us
    all_to_all x4, blocking collectives, on_device(): back = lax.all_to_all(att, ('z', 'x'), 0, 0, tiled=True)  45.8 us
    ppermute x4, waiting for transfers between devices, on_device(): recv = lax.ppermute(new, 'pipe', [(i, i + 1) for i in range(LAYERS - 1)])  22.9 us
    ppermute x5, waiting for transfers between devices, on_device(): oth = lax.ppermute(own, 'core', [(0, 1), (1, 0)])  10.8 us
    unnamed x31, local copies, waits for them, and re-layouts  8.15 us
    all_to_all x1, waiting for transfers between devices, on_device(): back = lax.all_to_all(att, ('z', 'x'), 0, 0, tiled=True)  6.66 us
    ppermute x4, starting transfers between devices, on_device(): recv = lax.ppermute(new, 'pipe', [(i, i + 1) for i in range(LAYERS - 1)])  5.17 us
  transfers between devices with their start and end apart: 10, of which 10 were waited for; matrix products, arithmetic and copies ran while one was open for 1% of the time, Pallas kernels for 0%

profile of v1, /device:TPU:24, one launch (start us, length us, event | category | flops | bytes accessed | tf_op | source)
XLA Modules:
  0.0 236.8 jit_solution(14326219307112450502)
XLA Ops:
  5.2 5.0 %copy-done = bf16[1,1536,4608]{2,1,0:T(8,128)(2,1)S(1)} copy-done((bf16[1,1536,4608]{2,1,0:T(8,128)(2,1)S(1)}, bf16[1,1536,4608]{2,1,0:T(8,128)(2,1)}, u32[]{:S(2)}) %copy-start) | copy-done | bytes 14155800
  10.2 6.0 %project0.1 = (bf16[16,288,128]{2,1,0:T(8,128)(2,1)S(1)}, bf16[48,3072]{1,0:T(8,128)(2,1)S(1)}) custom-call(s32[5]{0:T(128)S(1)} %pad_add_fusion.refs_0_.info_ref, bf16[4,24,1536]{2,1,0:T(8,128)(2,1)S(1)} %bitcast.7, f32[1,3,1536]{2,1,0:T(4,128)S(1)} %copy.14.refs_2_.refs_4_.refs_3_.refs_5_, bf16[1,1536,4608]{2,1,0:T(8,128)(2,1)S(1)} %copy-done, ...), custom_call_target="tpu_custom_call" | custom-call | tf_op jit(solution)/shard_map/project0/pallas_call | solution.py:239
  16.2 26.2 %all_to_all.50.refs_1_ = bf16[16,288,128]{2,1,0:T(8,128)(2,1)S(1)} all-to-all(bf16[16,288,128]{2,1,0:T(8,128)(2,1)S(1)} %get-tuple-element.24), channel_id=1, replica_groups=mesh['pipe'=4,'z'=4,'x'=4,'core'=2] {'z','x'}, dimensions={0} | all-to-all | bytes 2359296 | tf_op jit(solution)/shard_map/all_to_all | solution.py:272
  45.3 3.9 %attend0.1 = (bf16[16,48,128]{2,1,0:T(8,128)(2,1)S(1)}, bf16[4,768,128]{2,1,0:T(8,128)(2,1)S(1)}, bf16[4,768,128]{2,1,0:T(8,128)(2,1)S(1)}) custom-call(s32[5]{0:T(128)S(1)} %pad_add_fusion.refs_0_.info_ref, bf16[16,288,128]{2,1,0:T(8,128)(2,1)S(1)} %all_to_all.50.refs_1_, bf16[16,288,128]{2,1,0:T(8,128)(2,1)S(1)} %collective-permute-done.refs_2_), custom_call_target="tpu_custom_call" | custom-call | tf_op jit(solution)/shard_map/attend0/pallas_call | solution.py:239
  49.2 11.4 %all_to_all.51.refs_1_ = bf16[16,48,128]{2,1,0:T(8,128)(2,1)S(1)} all-to-all(bf16[16,48,128]{2,1,0:T(8,128)(2,1)S(1)} %get-tuple-element.25), channel_id=1, replica_groups=mesh['pipe'=4,'z'=4,'x'=4,'core'=2] {'z','x'}, dimensions={0} | all-to-all | bytes 393216 | tf_op jit(solution)/shard_map/all_to_all | solution.py:283
  63.4 5.7 %collective-permute-done.1.refs_2_.refs_4_ = bf16[48,1536]{1,0:T(8,128)(2,1)S(1)} collective-permute-done((bf16[48,1536]{1,0:T(8,128)(2,1)S(1)}, bf16[48,1536]{1,0:T(8,128)(2,1)S(1)}, u32[]{:S(2)}, u32[]{:S(2)}) %collective-permute-start.1) | collective-permute-done | bytes 147488 | tf_op jit(solution)/shard_map/ppermute | solution.py:295
  69.2 3.3 %project1.1 = (bf16[16,144,128]{2,1,0:T(8,128)(2,1)S(1)}, bf16[48,3072]{1,0:T(8,128)(2,1)S(1)}) custom-call(s32[5]{0:T(128)S(1)} %pad_add_fusion.refs_0_.info_ref, bf16[4,24,1536]{2,1,0:T(8,128)(2,1)S(1)} %bitcast.9, bf16[48,1536]{1,0:T(8,128)(2,1)S(1)} %collective-permute-done.1.refs_2_.refs_4_, f32[1,3,1536]{2,1,0:T(4,128)S(1)} %copy.14.refs_2_.refs_4_.refs_3_.refs_5_, ...), custom_call_target="tpu_custom_call" | custom-call | tf_op jit(solution)/shard_map/project1/pallas_call | solution.py:239
  72.5 13.5 %all_to_all.52.refs_1_ = bf16[16,144,128]{2,1,0:T(8,128)(2,1)S(1)} all-to-all(bf16[16,144,128]{2,1,0:T(8,128)(2,1)S(1)} %get-tuple-element.26), channel_id=1, replica_groups=mesh['pipe'=4,'z'=4,'x'=4,'core'=2] {'z','x'}, dimensions={0} | all-to-all | bytes 1179648 | tf_op jit(solution)/shard_map/all_to_all | solution.py:272
  88.0 3.8 %attend1.1 = (bf16[16,48,128]{2,1,0:T(8,128)(2,1)S(1)}, bf16[4,768,128]{2,1,0:T(8,128)(2,1)S(1)}, bf16[4,768,128]{2,1,0:T(8,128)(2,1)S(1)}) custom-call(s32[5]{0:T(128)S(1)} %pad_add_fusion.refs_0_.info_ref, bf16[16,144,128]{2,1,0:T(8,128)(2,1)S(1)} %all_to_all.52.refs_1_, bf16[16,144,128]{2,1,0:T(8,128)(2,1)S(1)} %collective-permute-done.2.refs_2_, ...), custom_call_target="tpu_custom_call" | custom-call | tf_op jit(solution)/shard_map/attend1/pallas_call | solution.py:239
  91.8 11.5 %all_to_all.53.refs_1_ = bf16[16,48,128]{2,1,0:T(8,128)(2,1)S(1)} all-to-all(bf16[16,48,128]{2,1,0:T(8,128)(2,1)S(1)} %get-tuple-element.29), channel_id=1, replica_groups=mesh['pipe'=4,'z'=4,'x'=4,'core'=2] {'z','x'}, dimensions={0} | all-to-all | bytes 393216 | tf_op jit(solution)/shard_map/all_to_all | solution.py:283
  106.1 5.7 %collective-permute-done.3.refs_2_.refs_4_ = bf16[48,1536]{1,0:T(8,128)(2,1)S(1)} collective-permute-done((bf16[48,1536]{1,0:T(8,128)(2,1)S(1)}, bf16[48,1536]{1,0:T(8,128)(2,1)S(1)}, u32[]{:S(2)}, u32[]{:S(2)}) %collective-permute-start.3) | collective-permute-done | bytes 147488 | tf_op jit(solution)/shard_map/ppermute | solution.py:295
  111.8 3.3 %project2.1 = (bf16[16,144,128]{2,1,0:T(8,128)(2,1)S(1)}, bf16[48,3072]{1,0:T(8,128)(2,1)S(1)}) custom-call(s32[5]{0:T(128)S(1)} %pad_add_fusion.refs_0_.info_ref, bf16[4,24,1536]{2,1,0:T(8,128)(2,1)S(1)} %bitcast.11, bf16[48,1536]{1,0:T(8,128)(2,1)S(1)} %collective-permute-done.3.refs_2_.refs_4_, f32[1,3,1536]{2,1,0:T(4,128)S(1)} %copy.14.refs_2_.refs_4_.refs_3_.refs_5_, ...), custom_call_target="tpu_custom_call" | custom-call | tf_op jit(solution)/shard_map/project2/pallas_call | solution.py:239
  115.1 13.5 %all_to_all.54.refs_1_ = bf16[16,144,128]{2,1,0:T(8,128)(2,1)S(1)} all-to-all(bf16[16,144,128]{2,1,0:T(8,128)(2,1)S(1)} %get-tuple-element.30), channel_id=1, replica_groups=mesh['pipe'=4,'z'=4,'x'=4,'core'=2] {'z','x'}, dimensions={0} | all-to-all | bytes 1179648 | tf_op jit(solution)/shard_map/all_to_all | solution.py:272
  130.6 3.8 %attend2.1 = (bf16[16,48,128]{2,1,0:T(8,128)(2,1)S(1)}, bf16[4,768,128]{2,1,0:T(8,128)(2,1)S(1)}, bf16[4,768,128]{2,1,0:T(8,128)(2,1)S(1)}) custom-call(s32[5]{0:T(128)S(1)} %pad_add_fusion.refs_0_.info_ref, bf16[16,144,128]{2,1,0:T(8,128)(2,1)S(1)} %all_to_all.54.refs_1_, bf16[16,144,128]{2,1,0:T(8,128)(2,1)S(1)} %collective-permute-done.4.refs_2_, ...), custom_call_target="tpu_custom_call" | custom-call | tf_op jit(solution)/shard_map/attend2/pallas_call | solution.py:239
  134.4 11.5 %all_to_all.55.refs_1_ = bf16[16,48,128]{2,1,0:T(8,128)(2,1)S(1)} all-to-all(bf16[16,48,128]{2,1,0:T(8,128)(2,1)S(1)} %get-tuple-element.33), channel_id=1, replica_groups=mesh['pipe'=4,'z'=4,'x'=4,'core'=2] {'z','x'}, dimensions={0} | all-to-all | bytes 393216 | tf_op jit(solution)/shard_map/all_to_all | solution.py:283
  148.7 5.7 %collective-permute-done.5.refs_2_.refs_4_ = bf16[48,1536]{1,0:T(8,128)(2,1)S(1)} collective-permute-done((bf16[48,1536]{1,0:T(8,128)(2,1)S(1)}, bf16[48,1536]{1,0:T(8,128)(2,1)S(1)}, u32[]{:S(2)}, u32[]{:S(2)}) %collective-permute-start.5) | collective-permute-done | bytes 147488 | tf_op jit(solution)/shard_map/ppermute | solution.py:295
  157.7 13.5 %all_to_all.56.refs_1_ = bf16[16,144,128]{2,1,0:T(8,128)(2,1)S(1)} all-to-all(bf16[16,144,128]{2,1,0:T(8,128)(2,1)S(1)} %get-tuple-element.34), channel_id=1, replica_groups=mesh['pipe'=4,'z'=4,'x'=4,'core'=2] {'z','x'}, dimensions={0} | all-to-all | bytes 1179648 | tf_op jit(solution)/shard_map/all_to_all | solution.py:272
  173.2 3.8 %attend3.1 = (bf16[16,48,128]{2,1,0:T(8,128)(2,1)S(1)}, bf16[4,768,128]{2,1,0:T(8,128)(2,1)S(1)}, bf16[4,768,128]{2,1,0:T(8,128)(2,1)S(1)}) custom-call(s32[5]{0:T(128)S(1)} %pad_add_fusion.refs_0_.info_ref, bf16[16,144,128]{2,1,0:T(8,128)(2,1)S(1)} %all_to_all.56.refs_1_, bf16[16,144,128]{2,1,0:T(8,128)(2,1)S(1)} %collective-permute-done.6.refs_2_, ...), custom_call_target="tpu_custom_call" | custom-call | tf_op jit(solution)/shard_map/attend3/pallas_call | solution.py:239
  177.0 11.5 %all_to_all.57.refs_1_ = bf16[16,48,128]{2,1,0:T(8,128)(2,1)S(1)} all-to-all(bf16[16,48,128]{2,1,0:T(8,128)(2,1)S(1)} %get-tuple-element.37), channel_id=1, replica_groups=mesh['pipe'=4,'z'=4,'x'=4,'core'=2] {'z','x'}, dimensions={0} | all-to-all | bytes 393216 | tf_op jit(solution)/shard_map/all_to_all | solution.py:283
  191.3 5.7 %collective-permute-done.7.refs_2_.refs_4_ = bf16[48,1536]{1,0:T(8,128)(2,1)S(1)} collective-permute-done((bf16[48,1536]{1,0:T(8,128)(2,1)S(1)}, bf16[48,1536]{1,0:T(8,128)(2,1)S(1)}, u32[]{:S(2)}, u32[]{:S(2)}) %collective-permute-start.7) | collective-permute-done | bytes 147488 | tf_op jit(solution)/shard_map/ppermute | solution.py:295
  200.4 13.5 %all_to_all.58.refs_1_ = bf16[16,144,128]{2,1,0:T(8,128)(2,1)S(1)} all-to-all(bf16[16,144,128]{2,1,0:T(8,128)(2,1)S(1)} %get-tuple-element.38), channel_id=1, replica_groups=mesh['pipe'=4,'z'=4,'x'=4,'core'=2] {'z','x'}, dimensions={0} | all-to-all | bytes 1179648 | tf_op jit(solution)/shard_map/all_to_all | solution.py:272
  215.8 4.3 %attend4.1 = bf16[16,48,128]{2,1,0:T(8,128)(2,1)} custom-call(s32[5]{0:T(128)S(1)} %pad_add_fusion.refs_0_.info_ref, bf16[16,144,128]{2,1,0:T(8,128)(2,1)S(1)} %all_to_all.58.refs_1_, bf16[16,144,128]{2,1,0:T(8,128)(2,1)S(1)} %collective-permute-done.8.refs_2_, bf16[4,768,128]{2,1,0:T(8,128)(2,1)S(1)} %get-tuple-element.39.refs_3_, ...), custom_call_target="tpu_custom_call" | custom-call | tf_op jit(solution)/shard_map/attend4/pallas_call | solution.py:239
  220.2 3.5 %all-to-all-start.9 = ((bf16[16,48,128]{2,1,0:T(8,128)(2,1)}), bf16[16,48,128]{2,1,0:T(8,128)(2,1)S(1)}, u32[]{:S(2)}, u32[]{:S(2)}) async-start(bf16[16,48,128]{2,1,0:T(8,128)(2,1)} %attend4.1), calls=%async_computation.9 | async-start | bytes 393216 | tf_op jit(solution)/shard_map/all_to_all | solution.py:283
  225.6 6.7 %all-to-all-done.9.refs_1_ = bf16[16,48,128]{2,1,0:T(8,128)(2,1)S(1)} async-done(((bf16[16,48,128]{2,1,0:T(8,128)(2,1)}), bf16[16,48,128]{2,1,0:T(8,128)(2,1)S(1)}, u32[]{:S(2)}, u32[]{:S(2)}) %all-to-all-start.9) | async-done | bytes 196640 | tf_op jit(solution)/shard_map/all_to_all | solution.py:283
  (64 shorter events, 39.4 us)
Async XLA Ops:
  0.6 4.2 %copy-start.4 = (pred[128]{0:T(512)(128)(4,1)S(1)}, pred[128]{0:T(512)(128)(4,1)}, u32[]{:S(2)}) copy-start(pred[128]{0:T(512)(128)(4,1)} %constant.27) | copy-start | bytes 388
  0.6 4.2 %copy-start.5 = (pred[128]{0:T(512)(128)(4,1)S(1)}, pred[128]{0:T(512)(128)(4,1)}, u32[]{:S(2)}) copy-start(pred[128]{0:T(512)(128)(4,1)} %constant.26) | copy-start | bytes 388
  0.7 4.2 %copy-start.6 = (pred[128]{0:T(512)(128)(4,1)S(1)}, pred[128]{0:T(512)(128)(4,1)}, u32[]{:S(2)}) copy-start(pred[128]{0:T(512)(128)(4,1)} %constant.25) | copy-start | bytes 388
  0.7 4.1 %copy-start.7 = (f32[128]{0:T(128)S(1)}, f32[128]{0:T(128)}, u32[]{:S(2)}) copy-start(f32[128]{0:T(128)} %constant.16.clone) | copy-start | bytes 1540
  0.7 4.0 %copy-start.8 = (s32[4]{0:T(128)S(1)}, s32[4]{0:T(128)}, u32[]{:S(2)}) copy-start(s32[4]{0:T(128)} %param.19) | copy-start | bytes 52
  0.7 4.4 %copy-start.3 = (f32[1,2,128]{2,1,0:T(2,128)S(1)}, f32[1,2,128]{2,1,0:T(2,128)}, u32[]{:S(2)}) copy-start(f32[1,2,128]{2,1,0:T(2,128)} %refs_5_.11) | copy-start | bytes 3076
  0.7 4.4 %copy-start.2 = (bf16[96,1536]{1,0:T(8,128)(2,1)S(1)}, bf16[96,1536]{1,0:T(8,128)(2,1)}, u32[]{:S(2)}) copy-start(bf16[96,1536]{1,0:T(8,128)(2,1)} %param.12) | copy-start | bytes 884740
  2.5 58.1 %slice-start.4 = ((s8[4718592]{0:T(1024)(128)(4,1)}), s8[524288]{0:T(1024)(128)(4,1)S(1)}, s32[]{:S(2)}) async-start(s8[4718592]{0:T(1024)(128)(4,1)} %bitcast.5), calls=%async_computation.14 | async-start | bytes 1048576
  5.1 5.0 %copy-start = (bf16[1,1536,4608]{2,1,0:T(8,128)(2,1)S(1)}, bf16[1,1536,4608]{2,1,0:T(8,128)(2,1)}, u32[]{:S(2)}) copy-start(bf16[1,1536,4608]{2,1,0:T(8,128)(2,1)} %refs_4_.10) | copy-start | bytes 42467332
  10.2 50.4 %slice-start.5 = ((s8[4718592]{0:T(1024)(128)(4,1)}), s8[4194304]{0:T(1024)(128)(4,1)S(1)}, s32[]{:S(2)}) async-start(s8[4718592]{0:T(1024)(128)(4,1)} %bitcast.5), calls=%async_computation.15 | async-start | bytes 8388608
  10.2 59.0 %slice-start = ((s8[14155776]{0:T(1024)(128)(4,1)}), s8[1572864]{0:T(1024)(128)(4,1)S(1)}, s32[]{:S(2)}) async-start(s8[14155776]{0:T(1024)(128)(4,1)} %bitcast.3), calls=%async_computation.10 | async-start | bytes 3145728
  10.2 59.0 %slice-start.1 = ((s8[14155776]{0:T(1024)(128)(4,1)}), s8[4194304]{0:T(1024)(128)(4,1)S(1)}, s32[]{:S(2)}) async-start(s8[14155776]{0:T(1024)(128)(4,1)} %bitcast.3), calls=%async_computation.11 | async-start | bytes 8388608
  10.2 59.0 %slice-start.2 = ((s8[14155776]{0:T(1024)(128)(4,1)}), s8[4194304]{0:T(1024)(128)(4,1)S(1)}, s32[]{:S(2)}) async-start(s8[14155776]{0:T(1024)(128)(4,1)} %bitcast.3), calls=%async_computation.12 | async-start | bytes 8388608
  42.4 26.7 %slice-start.3 = ((s8[14155776]{0:T(1024)(128)(4,1)}), s8[4194304]{0:T(1024)(128)(4,1)S(1)}, s32[]{:S(2)}) async-start(s8[14155776]{0:T(1024)(128)(4,1)} %bitcast.3), calls=%async_computation.13 | async-start | bytes 8388608
  42.4 2.8 %collective-permute-start = (bf16[16,288,128]{2,1,0:T(8,128)(2,1)S(1)}, bf16[16,288,128]{2,1,0:T(8,128)(2,1)S(1)}, u32[]{:S(2)}, u32[]{:S(2)}) collective-permute-start(bf16[16,288,128]{2,1,0:T(8,128)(2,1)S(1)} %all_to_all.50.refs_1_), channel_id=1, source_target_pairs={{0,1},{1,0},{2,3},{3,2},{4,5},{5,4},{6,7},{7,6},{8,9},{9,8},{10,11... | collective-permute-start | bytes 3538952 | tf_op jit(solution)/shard_map/ppermute | solution.py:273
  62.1 7.0 %collective-permute-start.1 = (bf16[48,1536]{1,0:T(8,128)(2,1)S(1)}, bf16[48,1536]{1,0:T(8,128)(2,1)S(1)}, u32[]{:S(2)}, u32[]{:S(2)}) collective-permute-start(bf16[48,1536]{1,0:T(8,128)(2,1)S(1)} %output0.1.refs_6_), channel_id=1, source_target_pairs={{0,32},{32,64},{64,96},{1,33},{33,65},{65,97},{2,34},{34,66},{66,9... | collective-permute-start | bytes 442376 | tf_op jit(solution)/shard_map/ppermute | solution.py:295
  86.0 2.0 collective-permute-start.2
  104.8 7.0 %collective-permute-start.3 = (bf16[48,1536]{1,0:T(8,128)(2,1)S(1)}, bf16[48,1536]{1,0:T(8,128)(2,1)S(1)}, u32[]{:S(2)}, u32[]{:S(2)}) collective-permute-start(bf16[48,1536]{1,0:T(8,128)(2,1)S(1)} %output1.1.refs_7_), channel_id=1, source_target_pairs={{0,32},{32,64},{64,96},{1,33},{33,65},{65,97},{2,34},{34,66},{66,9... | collective-permute-start | bytes 442376 | tf_op jit(solution)/shard_map/ppermute | solution.py:295
  128.6 2.0 collective-permute-start.4
  147.4 7.0 %collective-permute-start.5 = (bf16[48,1536]{1,0:T(8,128)(2,1)S(1)}, bf16[48,1536]{1,0:T(8,128)(2,1)S(1)}, u32[]{:S(2)}, u32[]{:S(2)}) collective-permute-start(bf16[48,1536]{1,0:T(8,128)(2,1)S(1)} %output2.1.refs_8_), channel_id=1, source_target_pairs={{0,32},{32,64},{64,96},{1,33},{33,65},{65,97},{2,34},{34,66},{66,9... | collective-permute-start | bytes 442376 | tf_op jit(solution)/shard_map/ppermute | solution.py:295
  171.2 2.0 collective-permute-start.6
  190.0 7.0 %collective-permute-start.7 = (bf16[48,1536]{1,0:T(8,128)(2,1)S(1)}, bf16[48,1536]{1,0:T(8,128)(2,1)S(1)}, u32[]{:S(2)}, u32[]{:S(2)}) collective-permute-start(bf16[48,1536]{1,0:T(8,128)(2,1)S(1)} %output3.1.refs_9_), channel_id=1, source_target_pairs={{0,32},{32,64},{64,96},{1,33},{33,65},{65,97},{2,34},{34,66},{66,9... | collective-permute-start | bytes 442376 | tf_op jit(solution)/shard_map/ppermute | solution.py:295
  213.8 2.0 collective-permute-start.8
  220.2 12.1 %all-to-all-start.9 = ((bf16[16,48,128]{2,1,0:T(8,128)(2,1)}), bf16[16,48,128]{2,1,0:T(8,128)(2,1)S(1)}, u32[]{:S(2)}, u32[]{:S(2)}) async-start(bf16[16,48,128]{2,1,0:T(8,128)(2,1)} %attend4.1), calls=%async_computation.9 | async-start | bytes 393216 | tf_op jit(solution)/shard_map/all_to_all | solution.py:283
  (1 other events, 2.3 us)
